TPU v7x, 32 devices: a whole 2x2x4 slice. The times are simulated.
32 devices in a mesh: dp: 16 (over z, x, core), chan: 2 (over y).
Axes of the slice: x: 2, y: 2, z: 4, core: 2. Of those that a mesh axis runs over, the one named last changes fastest.
Arguments:
- params: float32 [2, 2, 13696, 128], P('chan', None, 'dp'), may hold values from -6 to 6, as said below
- momentum: float32 [2, 2, 13696, 128], P('chan', None, 'dp'), may hold values from -1.5 to 1.5
- ema_params: float32 [2, 2, 13696, 128], P('chan', None, 'dp'), may hold values from -0.75 to 0.75
- latents: float32 [16, 4, 1024], P('dp'), may hold values from -6 to 6
- noise_eps: float32 [16, 4, 1024], P('dp'), may hold values from -6 to 6
- timesteps: int32 [16], P('dp'), may hold values from 0 to 999
- pixel_mask: int32 [16, 1024], P('dp'), may hold values from 0 to 1
- context: bfloat16 [16, 77, 768], P('dp'), may hold values from -6 to 6
Outputs:
- new_params: float32 [2, 2, 13696, 128], P('chan', None, 'dp')
- new_momentum: float32 [2, 2, 13696, 128], P('chan', None, 'dp')
- new_ema: float32 [2, 2, 13696, 128], P('chan', None, 'dp')
- loss_sum: float32 [], replicated
- pixel_count: float32 [], replicated
Inputs may be any that keep to these rules, and one draw needn't show every extreme that they name: `params`: weights about fan_in^-0.5 (self_out 8 times, cross_out 4 times that), gains about 1, biases about 0.1.
All inputs are finite; a program needn't handle non-finite values.
Results may differ from a plain program's by a relative error of at most 0.00096.
Values may be sent and summed in bfloat16 or wider, within the bound.
A program may use at most 448 MiB of HBM per device.

v0:
```python
import math
from functools import partial

import jax
import jax.numpy as jnp
from jax import lax
from jax.experimental import pallas as pl
from jax.experimental.pallas import tpu as pltpu
from jax.sharding import PartitionSpec as P

D = 320
W = 160
HEADS = 8
HD = 40
CTX = 768
TXT = 77
LAT = 4
SIDE = 32
N = 1024
EPS = 1e-5
LR = 0.2
MU = 0.9
ED = 0.9
CH = "chan"
DP = "dp"
F32 = jnp.float32
BF = jnp.bfloat16
HI = lax.Precision.HIGHEST
SCALE = HD**-0.5
LOG2E = 1.0 / math.log(2.0)

R0 = 4000
U1, U2, U3 = 2920, 4204, 9328
FRONT = 3650
T1, T2, T3 = 3650, 5255, 11660
C2 = 2
PI = 2885
QKV = 3208
SO = 4168
CQ = 4491
CKV = 4811
CO = 6347
GI = 6670
GIB = 9230
GO = 9238
PO = 10519
OUT = 10842
OUTB = 10878
R1 = 13600
VEC0 = (36, 37, 38, 2919)
VEC1 = (0, 1, 2882, 2883, 2884, 3205, 3206, 3207, 4488, 4489, 4490, 6667, 6668, 6669, 10518, 10839, 10840, 10841)
(N2G, N2B, C2B, NTG, NTB, PIB, L1G, L1B, SOB, L2G, L2B, COB, L3G, L3B, GOB, POB, NOG, NOB) = range(18)
MPI, MQ, MK, MV = range(4)
MSO, MCQ, MCO, MPO, MGV, MGG, MGO = 0, 1, 2, 3, 4, 8, 12


class Flow:
    def __init__(self, ins, outs, sems):
        self.ins = {i: pltpu.make_async_copy(src, dst, sems.at[j]) for j, (i, src, dst) in enumerate(ins)}
        n = len(ins)
        self.outs = {i: pltpu.make_async_copy(src, dst, sems.at[n + j]) for j, (i, dst, src) in enumerate(outs)}
        self.waiting = set(self.ins)
        self.going = []
        for copy in self.ins.values():
            copy.start()

    def need(self, *which):
        for i in which:
            self.ins[i].wait()
            self.waiting.discard(i)

    def ready(self, *which):
        for i in which:
            self.outs[i].start()
            self.going.append(i)

    def end(self):
        self.need(*sorted(self.waiting))
        self.ready(*(i for i in self.outs if i not in self.going))
        for copy in self.outs.values():
            copy.wait()


def kcall(body, outs, ins, scratch=(), late=(), early=()):
    vm, hbm = pl.BlockSpec(memory_space=pltpu.VMEM), pl.BlockSpec(memory_space=pl.ANY)
    single = not isinstance(outs, tuple)
    outs = (outs,) if single else outs
    n, m = len(ins), len(outs)
    late, early = tuple(late), tuple(early)
    scratch = list(scratch)
    count = len(scratch)
    if late or early:
        scratch += [pltpu.VMEM(ins[i].shape, ins[i].dtype) for i in late]
        scratch += [pltpu.VMEM(outs[i].shape, outs[i].dtype) for i in early]
        scratch.append(pltpu.SemaphoreType.DMA((len(late) + len(early),)))

    def whole(*refs):
        if not (late or early):
            return body(*refs)
        given, made, rest = list(refs[:n]), list(refs[n : n + m]), refs[n + m :]
        kept = rest[count:-1]
        inward = [(i, given[i], kept[j]) for j, i in enumerate(late)]
        outward = [(i, made[i], kept[len(late) + j]) for j, i in enumerate(early)]
        for i, _, ref in inward:
            given[i] = ref
        for i, _, ref in outward:
            made[i] = ref
        flow = Flow(inward, outward, rest[-1])
        body(flow, *given, *made, *rest[:count])
        flow.end()

    done = pl.pallas_call(
        whole,
        out_shape=outs,
        in_specs=[hbm if i in late else vm for i in range(n)],
        out_specs=tuple(hbm if i in early else vm for i in range(m)),
        scratch_shapes=scratch,
        compiler_params=pltpu.CompilerParams(vmem_limit_bytes=63 * 2**20),
    )(*ins)
    return done[0] if single else done


def sds(shape, dtype=F32):
    return jax.ShapeDtypeStruct(shape, dtype)


def tiles(fn, size=256, total=N):
    for t in range(total // size):
        fn(pl.ds(t * size, size))


def nn(a, b):
    return jnp.dot(a, b, preferred_element_type=F32)


def nt(a, b):
    return lax.dot_general(a, b, (((1,), (1,)), ((), ())), preferred_element_type=F32)


def tn(a, b):
    return lax.dot_general(a, b, (((0,), (0,)), ((), ())), preferred_element_type=F32)


def colsum(v):
    return jnp.sum(v, axis=0, keepdims=True)


def flatten(a_ref, flat, rows):
    for b in range(2):
        for t in range(a_ref.shape[1]):
            flat[b, t * rows : (t + 1) * rows, :] = a_ref[b, t, :rows, :].astype(F32)


def unroll(flat, s_ref, lo_chunk, hi_chunk):
    q = 80

    @pl.loop(lo_chunk, hi_chunk)
    def _(c):
        f = [[flat[b, pl.ds(c * 5 * q + j, q, stride=5), :] for j in range(5)] for b in range(2)]
        for i in range(4):
            row = []
            for b in range(2):
                lo = 32 * i
                first, second = f[b][i], f[b][i + 1]
                row += [first[:, lo:], second[:, : lo + 32]] if lo else [first, second[:, :32]]
            full = jnp.concatenate(row, axis=1)
            for k, (lo, hi) in enumerate(((0, 128), (128, 256), (256, 320))):
                s_ref[k, pl.ds(c * 4 * q + i, q, stride=4), : hi - lo] = full[:, lo:hi]


def get_rows(s_ref, start, count, step=1):
    ds = pl.ds(start, count) if step == 1 else pl.ds(start, count, stride=step)
    return jnp.concatenate([s_ref[0, ds, :], s_ref[1, ds, :], s_ref[2, ds, :64]], axis=1)


def put_taps(s_ref, start, w, back):
    for r in range(3):
        taps = [get_rows(s_ref, start + D * (3 * r + i), D).astype(BF) for i in range(3)]
        for i in range(3):
            w[r, D * i : D * (i + 1), :] = taps[i]
        back[r] = jnp.concatenate(taps[::-1], axis=1)


def unit_row(parts):
    out = [p[:, W * b : W * (b + 1)] for b in range(2) for p in parts]
    return jnp.broadcast_to(jnp.concatenate(out, axis=1), (8, 4 * D))


def unit_parts(row):
    return [
        jnp.concatenate([row[:, W * i : W * (i + 1)], row[:, 640 + W * i : 640 + W * (i + 1)]], axis=1)
        for i in range(4)
    ]


def take_front(s_ref, win, w1, w1b, vec):
    win[...] = get_rows(s_ref, 0, 36).astype(BF)
    put_taps(s_ref, 39, w1, w1b)
    for i, r in enumerate(VEC0):
        vec[i : i + 1, :] = get_rows(s_ref, r, 1)


def take_time(s_ref, tw2, tw3):
    for i in range(4):
        tw2[i] = get_rows(s_ref, U2 + i, 4 * D, 4).astype(BF)
    tw3[...] = get_rows(s_ref, U3, 4 * D).astype(BF)


def time_forward(s_ref, e, tw2, tw3, tv, p1, p2):
    u = e[...].astype(BF)
    p1[...] = unit_row(
        [nn(u, get_rows(s_ref, U1 + i, D, 4).astype(BF))[:1] + get_rows(s_ref, U1 + 4 * D + i, 1) for i in range(4)]
    )
    u = silu(p1[...]).astype(BF)
    p2[...] = unit_row([nn(u, tw2[i])[:1] + get_rows(s_ref, U2 + 16 * D + i, 1) for i in range(4)])
    u = silu(p2[...]).astype(BF)
    tv[...] = nn(u, tw3[...])[:1] + get_rows(s_ref, U3 + 4 * D, 1)


def unpack0_kernel(rows, a_ref, e, win, w1, w1b, vec, tw2, tw3, tv, p1, p2, flat, s_ref):
    flatten(a_ref, flat, rows)
    unroll(flat, s_ref, 0, R1 // 400)
    take_front(s_ref, win, w1, w1b, vec)
    take_time(s_ref, tw2, tw3)
    time_forward(s_ref, e, tw2, tw3, tv, p1, p2)


FE, FU1, FU2, FD1, FD2, FD3, FL = 0, 3, 13, 23, 28, 33, 35
FACTS = 40


def time_back(dtv, tw2, tw3, p1, p2, e, mask, loss, facts):
    g = jnp.broadcast_to(dtv[...], (8, D)).astype(BF)
    d2 = nt(g, tw3[...]) * silu_slope(p2[...])
    total = jnp.zeros((8, 4 * D), F32)
    for i, part in enumerate(unit_parts(d2)):
        total += nt(part.astype(BF), tw2[i])
    d1 = total * silu_slope(p1[...])
    put_facts(facts, e, p1, p2, d1, d2, dtv, mask, loss)


def put_facts(facts, e, p1, p2, d1, d2, dtv, mask, loss):
    first = lax.axis_index(CH) == 0
    facts[...] = jnp.zeros_like(facts)

    def put(at, v):
        for i in range(0, v.shape[1], 128):
            n = min(128, v.shape[1] - i)
            facts[at + i // 128 : at + i // 128 + 1, :n] = v[:1, i : i + n]

    put(FE, e[...].astype(BF).astype(F32))
    put(FU1, silu(p1[...]).astype(BF).astype(F32))
    put(FU2, silu(p2[...]).astype(BF).astype(F32))
    put(FD1, jnp.where(first, d1[:, : 2 * D], d1[:, 2 * D :]))
    put(FD2, jnp.where(first, d2[:, : 2 * D], d2[:, 2 * D :]))
    put(FD3, own(dtv[...]))
    facts[FL : FL + 1, 0:1] = loss[...]
    facts[FL : FL + 1, 1:2] = jnp.sum(mask[...].astype(F32), axis=1, keepdims=True)


def unpack1_kernel(rows, a_ref, c2, c2b, tr, mats, kv, vec, gib, wout, outb, flat, s_ref, o_ref):
    flatten(a_ref, flat, rows)
    unroll(flat, s_ref, 0, R1 // 400)
    put_taps(s_ref, C2, c2, c2b)
    tr[MPI] = get_rows(s_ref, PI, D).astype(BF)
    for m, r in ((MSO, SO), (MCQ, CQ), (MCO, CO), (MPO, PO)):
        mats[m] = get_rows(s_ref, r, D).astype(BF)
    for j in range(3):
        tr[MQ + j] = get_rows(s_ref, QKV + j, D, 3).astype(BF)
    for j in range(8):
        mats[MGV + j] = get_rows(s_ref, GI + j, D, 8).astype(BF)
    for j in range(4):
        for b in range(2):
            mats[MGO + j, b * W : (b + 1) * W, :] = get_rows(s_ref, GO + 640 * b + W * j, W).astype(BF)
    for j in range(2):
        kv[j] = get_rows(s_ref, CKV + j, CTX, 2).astype(BF)
    for i, r in enumerate(VEC1):
        vec[i : i + 1, :] = get_rows(s_ref, r, 1)
    gib[...] = get_rows(s_ref, GIB, 8)
    outb[...] = get_rows(s_ref, OUTB, 1)
    lane = lax.broadcasted_iota(jnp.int32, (W, W), 0)
    col = lax.broadcasted_iota(jnp.int32, (W, W), 1)
    pick = ((lane % 2) * 80 + lane // 2 == col).astype(BF)
    raw = get_rows(s_ref, OUT, 36).astype(BF)
    for b in range(2):
        moved = nn(raw[:, W * b : W * (b + 1)], pick)
        o_ref[0, :36, :] = moved[:, :128]
        o_ref[1, :36, :32] = moved[:, 128:]
        for ch in range(2):
            pieces = []
            for m in range(4):
                ds = pl.ds(m, 9, stride=4)
                both = jnp.concatenate([o_ref[0, ds, :], o_ref[1, ds, :32]], axis=1)
                pieces.append(both[:, 80 * ch : 80 * ch + 80])
            at = (2 * b + ch) * 9
            wout[at : at + 9, :] = jnp.concatenate(pieces, axis=1).astype(BF)


def pixel_col(n, axis):
    shape = (n, 1) if axis == 0 else (1, n)
    return lax.broadcasted_iota(jnp.int32, shape, axis)


def shift_lanes(v, tap):
    r, s = tap // 3 - 1, tap % 3 - 1
    pix = pixel_col(N, 1)
    i, j = pix // SIDE + r, pix % SIDE + s
    ok = (i >= 0) & (i < SIDE) & (j >= 0) & (j < SIDE)
    move = -(r * SIDE + s) % N
    moved = pltpu.roll(v, move, 1) if move else v
    return jnp.where(ok, moved, 0.0)


def put_shifts(ref, v):
    j = pixel_col(N, 0) % SIDE
    left = jnp.where(j == 0, 0.0, pltpu.roll(v, 1, 0)).astype(BF)
    right = jnp.where(j == SIDE - 1, 0.0, pltpu.roll(v, N - 1, 0)).astype(BF)
    ref[SIDE : SIDE + N, :] = jnp.concatenate([left, v.astype(BF), right], axis=1)


def clear_margins(ref):
    zero = jnp.zeros((SIDE, ref.shape[1]), BF)
    ref[:SIDE, :] = zero
    ref[SIDE + N :, :] = zero


def conv_rows(ref, w_ref):
    return sum(nn(ref[SIDE * r : SIDE * r + N, :], w_ref[r]) for r in range(3))


def conv_back_rows(ref, w_ref):
    return sum(nt(ref[SIDE * (2 - r) : SIDE * (2 - r) + N, :], w_ref[r]) for r in range(3))


def group_mean(sums):
    a = lax.broadcasted_iota(jnp.int32, (D, D), 0) // 10
    b = lax.broadcasted_iota(jnp.int32, (D, D), 1) // 10
    pool = jnp.where(a == b, 1.0, 0.0)
    wide = jnp.broadcast_to(sums, (8, D))
    out = jnp.dot(wide, pool, precision=HI, preferred_element_type=F32)
    return out[:1] * (1.0 / (10 * N))


def group_stats(v_ref, acc, sums):
    mean = group_mean(sums)
    acc[0:1, :] = colsum(jnp.square(v_ref[...] - mean))
    return mean, lax.rsqrt(group_mean(acc[0:1, :]) + EPS)


def silu(v):
    return v * jax.nn.sigmoid(v)


def silu_slope(v):
    sig = jax.nn.sigmoid(v)
    return sig * (1.0 + v * (1.0 - sig))


def layer(v):
    mean = jnp.sum(v, axis=1, keepdims=True) * (1.0 / D)
    sq = jnp.sum(v * v, axis=1, keepdims=True) * (1.0 / D)
    inv = lax.rsqrt(sq - mean * mean + EPS)
    return (v - mean) * inv, inv


def layer_back(grad, normed, inv, gain):
    ghat = grad * gain
    m1 = jnp.sum(ghat, axis=1, keepdims=True) * (1.0 / D)
    m2 = jnp.sum(ghat * normed, axis=1, keepdims=True) * (1.0 / D)
    return inv * (ghat - m1 - normed * m2)


def own(v):
    return jnp.where(lax.axis_index(CH) == 0, v[..., :W], v[..., W:])


def head(v, h):
    return v[:, HD * h : HD * (h + 1)]


def group_norm(src, acc, total, stats, at):
    mean, inv = group_stats(src, acc, total)
    stats[at : at + 1, :], stats[at + 1 : at + 2, :] = mean, inv
    return (src[...] - mean) * inv


def start_steps(noisy, tv, win, w1, vec0, h0, h1, a1, stats, sh, acc):
    def first():
        cols = jnp.concatenate([shift_lanes(noisy[...], t) for t in range(9)], axis=0).astype(BF)
        clear_margins(sh)
        stats[...] = jnp.zeros_like(stats)
        h = tn(cols, win[...]) + vec0[0:1, :]
        h0[...] = h
        y = silu(group_norm(h0, acc, colsum(h), stats, 0) * vec0[1:2, :] + vec0[2:3, :])
        put_shifts(sh, y)
        a1[...] = y.astype(BF)

    def taps(r):
        def one():
            part = nn(sh[SIDE * r : SIDE * r + N, :], w1[r])
            if r == 2:
                part += tv[...]
            h1[...] = (h1[...] if r else vec0[3:4, :]) + part

        return one

    return [first, taps(0), taps(1), taps(2)]


def start_kernel(noisy, tv, win, w1, vec0, h0, h1, a1, stats, sh, acc):
    for step in start_steps(noisy, tv, win, w1, vec0, h0, h1, a1, stats, sh, acc):
        step()


def front_kernel(flow, h0, h1, stats_in, c2, tr, vec1, h2, z0, a2, ntr, x1, q, k, v, stats, sh, acc):
    clear_margins(sh)
    stats[...] = stats_in[...]
    y = silu(group_norm(h1, acc, colsum(h1[...]), stats, 2) * vec1[N2G : N2G + 1, :] + vec1[N2B : N2B + 1, :])
    put_shifts(sh, y)
    a2[...] = y.astype(BF)
    flow.ready(2)
    flow.need(0, 3)
    h = h0[...] + conv_rows(sh, c2) + vec1[C2B : C2B + 1, :]
    h2[...] = h
    flow.ready(0)
    n = group_norm(h2, acc, colsum(h), stats, 4)
    n = (n * vec1[NTG : NTG + 1, :] + vec1[NTB : NTB + 1, :]).astype(BF)
    ntr[...] = n
    flow.ready(3)
    flow.need(4)
    z = nn(n, tr[MPI]) + vec1[PIB : PIB + 1, :]
    z0[...] = z
    flow.ready(1)
    normed, _ = layer(z)
    x = (normed * vec1[L1G : L1G + 1, :] + vec1[L1B : L1B + 1, :]).astype(BF)
    x1[...] = x
    flow.ready(4)
    for i, (at, dst) in enumerate(((MQ, q), (MK, k), (MV, v))):
        y = nn(x, tr[at]).astype(BF)
        for hd in range(HEADS):
            dst[hd] = head(y, hd)
        flow.ready(5 + i)


AT = 512


def attend_kernel(q, k, v, o, lse, ot):
    steps = [(h, pl.ds(t * AT, AT)) for h in range(HEADS) for t in range(N // AT)]

    def scores(h, rows):
        return nt(k[h], q[h, rows, :])

    now = scores(*steps[0])
    for i, (h, rows) in enumerate(steps):
        later = scores(*steps[i + 1]) if i + 1 < len(steps) else None
        if i % (N // AT) == 0:
            vt = v[h].astype(F32).T.astype(BF)
        s = now * (SCALE * LOG2E)
        top = jnp.max(s, axis=0, keepdims=True)
        e = jnp.exp2(s - top)
        total = jnp.sum(e, axis=0, keepdims=True)
        lse[h, :, rows] = top + jnp.log(total) * LOG2E
        ot[h * HD : (h + 1) * HD, rows] = nn(vt, (e * (1.0 / total)).astype(BF))
        now = later
    o[...] = ot[...].T.astype(BF)


KEYS = 128


def by_head(v):
    wide = jnp.concatenate([v, jnp.zeros((KEYS - TXT, D), v.dtype)], axis=0)
    col = lax.broadcasted_iota(jnp.int32, (KEYS, D), 1) // HD
    return jnp.concatenate([jnp.where(col == h, wide, 0.0) for h in range(HEADS)], axis=0)


def from_heads(vt):
    row = lax.broadcasted_iota(jnp.int32, (D, KEYS), 0) // HD
    total = jnp.zeros((D, KEYS), F32)
    for h in range(HEADS):
        total += jnp.where(row == h, vt[:, KEYS * h : KEYS * (h + 1)], 0.0)
    return total.T[:TXT]


def transposed(v):
    return v.T


def middle_kernel(
    flow, o, z0, h2, ctx, noise, mask, mats, kvw, vec, gib, wout, outb,
    dz1, dh3, dos, loss, gd, ggi, ggo, gkv, dvec, dgib, dwout, dbout,
    z1, z2, h3, x2, x3, oc, z3b, gl, by_a, by_g, a3, qc, kb, vb, prob, dsc, acc, pt, oct_, x2t, ot, x3t,
):
    def row(i):
        return vec[i : i + 1, :]

    def put(i, v):
        dvec[i : i + 1, :] = v

    flow.need(7)
    kb[...] = by_head(nn(ctx[...], kvw[0])).astype(BF)
    vb[...] = by_head(nn(ctx[...], kvw[1])).astype(BF)
    flow.need(6, 1)
    z = z0[...] + nn(o[...], mats[MSO]) + row(SOB)
    z1[...] = z
    normed, _ = layer(z)
    x = (normed * row(L2G) + row(L2B)).astype(BF)
    x2[...] = x
    qq = nn(x, mats[MCQ]).astype(BF)
    qc[...] = qq
    s = nt(qq, kb[...]) * (SCALE * LOG2E)
    there = lax.broadcasted_iota(jnp.int32, (1, KEYS), 1) < TXT
    for h in range(HEADS):
        at = slice(KEYS * h, KEYS * (h + 1))
        sh = jnp.where(there, s[:, at], -jnp.inf)
        e = jnp.exp2(sh - jnp.max(sh, axis=1, keepdims=True))
        prob[:, at] = e * (1.0 / jnp.sum(e, axis=1, keepdims=True))
    c = nn(prob[...].astype(BF), vb[...]).astype(BF)
    oc[...] = c
    z = z1[...] + nn(c, mats[MCO]) + row(COB)
    z2[...] = z
    normed, _ = layer(z)
    x = (normed * row(L3G) + row(L3B)).astype(BF)
    x3[...] = x
    moving = ((oc, oct_), (x2, x2t), (o, ot), (x3, x3t))
    for j in range(4):
        moving[j][1][...] = transposed(moving[j][0][...])
        a = nn(x, mats[MGV + j]) + gib[j : j + 1, :]
        g = nn(x, mats[MGG + j]) + gib[4 + j : 5 + j, :]
        cdf = 0.5 * (1.0 + lax.erf(g * math.sqrt(0.5)))
        gelu = g * cdf
        by_a[j] = gelu
        by_g[j] = a * (cdf + g * jnp.exp(-0.5 * g * g) * (1.0 / math.sqrt(2.0 * math.pi)))
        y = (a * gelu).astype(BF)
        gl[j] = y
        z = z + nn(y, mats[MGO + j])
    zb = (z + row(GOB)).astype(BF)
    z3b[...] = zb
    flow.need(2)
    h = h2[...] + nn(zb, mats[MPO]) + row(POB)
    h3[...] = h
    mean, inv = group_stats(h3, acc, colsum(h))
    gain, bias = row(NOG), row(NOB)
    a3[...] = silu((h3[...] - mean) * inv * gain + bias).astype(BF)
    taps = nt(wout[...], a3[...])
    for ch in range(LAT):
        pred = jnp.zeros((1, N), F32)
        for t in range(9):
            pred += shift_lanes(taps[9 * ch + t : 9 * ch + t + 1, :], t)
        at = W * (ch // 2) + ch % 2
        err = pred + outb[0:1, at : at + 1] - noise[ch : ch + 1, :]
        weighed = mask[...].astype(F32) * err
        g = 2.0 * weighed
        acc[2 + ch : 3 + ch, 0:1] = jnp.sum(weighed * err, axis=1, keepdims=True)
        dbout[ch : ch + 1, :] = jnp.broadcast_to(jnp.sum(g, axis=1, keepdims=True), (1, 128))
        for t in range(9):
            pt[9 * ch + t : 9 * ch + t + 1, :] = shift_lanes(g, 8 - t)
    loss[...] = acc[2:3, 0:1] + acc[3:4, 0:1] + acc[4:5, 0:1] + acc[5:6, 0:1]

    dvec[...] = jnp.zeros_like(dvec)
    taps = pt[...].astype(BF)
    dwout[...] = nn(taps, a3[...])
    n = (h3[...] - mean) * inv
    g = tn(taps, wout[...]) * silu_slope(n * gain + bias)
    dgain, dbias = colsum(g * n), colsum(g)
    put(NOG, dgain)
    put(NOB, dbias)
    g = inv * (g * gain - group_mean(gain * dbias) - n * group_mean(gain * dgain))
    dh3[...] = g
    flow.ready(1)
    put(POB, colsum(g))
    gd[0] = nn(transposed(z3b[...]), own(g).astype(BF)).astype(BF)
    dz3 = nt(g.astype(BF), mats[MPO])
    z1b = dz3.astype(BF)
    put(GOB, colsum(dz3))
    mine_t = transposed(own(dz3).astype(BF))
    xt = x3t[...]
    dx = jnp.zeros((N, D), F32)
    for j in range(4):
        dgl = nt(z1b, mats[MGO + j])
        ggo[j] = nn(mine_t, gl[j]).T.astype(BF)
        da = dgl * by_a[j]
        dg = dgl * by_g[j]
        dgib[j : j + 1, :] = colsum(da)
        dgib[4 + j : 5 + j, :] = colsum(dg)
        ggi[j] = nn(xt, own(da).astype(BF)).astype(BF)
        ggi[4 + j] = nn(xt, own(dg).astype(BF)).astype(BF)
        dx += nt(da.astype(BF), mats[MGV + j]) + nt(dg.astype(BF), mats[MGG + j])
    flow.ready(5, 6)
    normed, li = layer(z2[...])
    put(L3G, colsum(dx * normed))
    put(L3B, colsum(dx))
    dz = dz3 + layer_back(dx, normed, li, row(L3G))
    z2[...] = dz
    put(COB, colsum(dz))
    gd[1] = nn(oct_[...], own(dz).astype(BF)).astype(BF)
    do = nt(dz.astype(BF), mats[MCO]).astype(BF)
    dp = nt(do, vb[...])
    dot = transposed(do)
    qt = transposed(qc[...])
    gkv[1] = tn(ctx[...], own(from_heads(nn(dot, prob[...].astype(BF)))).astype(BF)).astype(BF)
    for h in range(HEADS):
        at = slice(KEYS * h, KEYS * (h + 1))
        p, d = prob[:, at], dp[:, at]
        dsc[:, at] = (p * (d - jnp.sum(p * d, axis=1, keepdims=True)) * SCALE).astype(BF)
    gkv[0] = tn(ctx[...], own(from_heads(nn(qt, dsc[...]))).astype(BF)).astype(BF)
    flow.ready(7)
    dq = nn(dsc[...], kb[...])
    gd[2] = nn(x2t[...], own(dq).astype(BF)).astype(BF)
    dx = nt(dq.astype(BF), mats[MCQ])
    normed, li = layer(z1[...])
    put(L2G, colsum(dx * normed))
    put(L2B, colsum(dx))
    dz = z2[...] + layer_back(dx, normed, li, row(L2G))
    dz1[...] = dz
    flow.ready(0)
    put(SOB, colsum(dz))
    gd[3] = nn(ot[...], own(dz).astype(BF)).astype(BF)
    do = nt(dz.astype(BF), mats[MSO]).astype(BF)
    for h in range(HEADS):
        dos[h] = head(do, h)


ABT = 256


def attend_back_kernel(q, k, v, do, lse, dq, dk, dv, qt, kacc, vacc):
    steps = [(h, pl.ds(t * ABT, ABT)) for h in range(HEADS) for t in range(N // ABT)]

    def scores(h, rows):
        return nt(k[h], q[h, rows, :]), nt(v[h], do[h, rows, :])

    now = scores(*steps[0])
    for i, (h, rows) in enumerate(steps):
        later = scores(*steps[i + 1]) if i + 1 < len(steps) else None
        s, dp = now
        p = jnp.exp2(s * (SCALE * LOG2E) - lse[h, :, rows])
        ds = (p * (dp - jnp.sum(p * dp, axis=0, keepdims=True)) * SCALE).astype(BF)
        dkt, dvt = nn(ds, q[h, rows, :]), nn(p.astype(BF), do[h, rows, :])
        if i % (N // ABT) == 0:
            kt = k[h].astype(F32).T.astype(BF)
            kacc[h], vacc[h] = dkt, dvt
        else:
            kacc[h] += dkt
            vacc[h] += dvt
        qt[h * HD : (h + 1) * HD, rows] = nn(kt, ds)
        now = later

    dq[...] = qt[...].T.astype(BF)

    def one(rows):
        for acc, dst in ((kacc, dk), (vacc, dv)):
            dst[rows, :] = jnp.concatenate([acc[h, rows, :] for h in range(HEADS)], axis=1).astype(BF)

    tiles(one)


def put_rows(s_ref, start, v, step=1):
    n = v.shape[0]
    ds = pl.ds(start, n) if step == 1 else pl.ds(start, n, stride=step)
    s_ref[0, ds, :] = v[:, :128]
    s_ref[1, ds, :32] = v[:, 128:]


def roll_rows(s_ref, out_ref, lo_chunk, hi_chunk):
    q = 80

    @pl.loop(lo_chunk, hi_chunk)
    def _(c):
        g = []
        for i in range(4):
            ds = pl.ds(c * 4 * q + i, q, stride=4)
            g.append((s_ref[0, ds, :], s_ref[1, ds, :32]))
        base = (c - lo_chunk) * 5 * q
        out_ref[pl.ds(base, q, stride=5), :] = g[0][0]
        for i in range(3):
            lo = 96 - 32 * i
            out_ref[pl.ds(base + i + 1, q, stride=5), :] = jnp.concatenate(
                ([g[i][0][:, 128 - 32 * i :]] if i else []) + [g[i][1], g[i + 1][0][:, :lo]], axis=1
            )
        out_ref[pl.ds(base + 4, q, stride=5), :] = jnp.concatenate([g[3][0][:, 32:], g[3][1]], axis=1)


def by_owner(s_ref, flat, out, total):
    owners, room = math.prod(out.shape[:-2]), out.shape[-2]
    size = room if total < owners * room and len(out.shape) == 3 else min(room, ROWS)
    half = owners // 2 * size
    for lo, hi, first in ((0, min(-(-half // 400), total // 400), 0), (half // 400, total // 400, owners // 2)):
        if hi > lo:
            roll_rows(s_ref, flat, lo, hi)
        at = 400 * max(hi - lo, 0)
        if at < flat.shape[0]:
            flat[at:, :] = jnp.zeros((flat.shape[0] - at, 128), F32)
        for t in range(first, first + owners // 2):
            spot = (t % 2, t // 2) if len(out.shape) == 4 else (t,)
            row = t * size - 400 * lo
            out[(*spot, slice(0, size))] = flat[row : row + size, :].astype(BF)
            if room > size:
                out[(*spot, slice(size, room))] = jnp.zeros((room - size, 128), BF)


def conv_grads(a_ref, g_ref, s_ref, start):
    at = transposed(a_ref[...])
    for r in range(3):
        rows = SIDE * (2 - r)
        three = nn(at, g_ref[rows : rows + N, :])
        for i in range(3):
            put_rows(s_ref, start + D * (3 * r + i), three[:, W * (2 - i) : W * (3 - i)])


def back_kernel(
    flow, dq, dk, dv, dz1, dh3, z0, h2, h1, h0, stats, w1, c2, tr, vec0, vec1, a1, a2, ntr, x1, noisy,
    gd, ggi, ggo, gkv, dvec_in, dgib, dwout, dbout,
    out1, out0, dtv,
    dh, g_ref, go_ref, dvec, s_ref, flat, o_ref,
):
    c = lax.axis_index(CH)
    clear_margins(g_ref)
    clear_margins(go_ref)
    dvec[...] = dvec_in[...]

    def row(i):
        return vec1[i : i + 1, :]

    def put(i, v):
        dvec[i : i + 1, :] = v

    dx = nt(dq[...], tr[MQ]) + nt(dk[...], tr[MK]) + nt(dv[...], tr[MV])
    xt = transposed(x1[...])
    for j, g in enumerate((dq, dk, dv)):
        put_rows(s_ref, QKV + j, nn(xt, own(g[...].astype(F32)).astype(BF)), 3)
    flow.need(5, 3)
    normed, li = layer(z0[...])
    put(L1G, colsum(dx * normed))
    put(L1B, colsum(dx))
    dz = dz1[...] + layer_back(dx, normed, li, row(L1G))
    put(PIB, colsum(dz))
    flow.need(17)
    put_rows(s_ref, PI, tn(ntr[...], own(dz).astype(BF)))
    g = nt(dz.astype(BF), tr[MPI])

    def norm_back(g, n, at, gain):
        dgain, dbias = colsum(g * n), colsum(g)
        back = stats[at + 1 : at + 2, :] * (g * gain - group_mean(gain * dbias) - n * group_mean(gain * dgain))
        return back, dgain, dbias

    def normed_of(src, at):
        return (src[...] - stats[at : at + 1, :]) * stats[at + 1 : at + 2, :]

    flow.need(6, 4)
    g, dgain, dbias = norm_back(g, normed_of(h2, 4), 4, row(NTG))
    put(NTG, dgain)
    put(NTB, dbias)
    g = dh3[...] + g
    dh[...] = g
    put(C2B, colsum(g))
    put_shifts(g_ref, g)
    put_shifts(go_ref, own(g))
    flow.need(16)
    conv_grads(a2, go_ref, s_ref, C2)
    flow.need(7, 11)
    n = normed_of(h1, 2)
    g = conv_back_rows(g_ref, c2) * silu_slope(n * row(N2G) + row(N2B))
    g, dgain, dbias = norm_back(g, n, 2, row(N2G))
    put(N2G, dgain)
    put(N2B, dbias)
    total = colsum(g)
    dtv[...] = total
    put_shifts(g_ref, g)
    put_shifts(go_ref, own(g))

    flow.need(20, 21, 22, 23)
    for i, r in enumerate((PO, CO, CQ, SO)):
        put_rows(s_ref, r, gd[i].astype(F32))
    for j in range(8):
        put_rows(s_ref, GI + j, ggi[j].astype(F32), 8)
    for j in range(4):
        rows = ggo[j].astype(F32)
        for b in range(2):
            put_rows(s_ref, GO + 640 * b + W * j, rows[W * b : W * (b + 1), :])
    for j in range(2):
        put_rows(s_ref, CKV + j, gkv[j].astype(F32), 2)
    for i, r in enumerate(VEC1):
        put_rows(s_ref, r, own(dvec[i : i + 1, :]))
    put_rows(s_ref, GIB, own(dgib[...]))
    wide = jnp.where(c == 0, dwout[:18, :], dwout[18:36, :])
    for ch in range(2):
        for m in range(4):
            o_ref[ch, pl.ds(m, 9, stride=4), :80] = wide[9 * ch : 9 * ch + 9, 80 * m : 80 * m + 80]
    lane = lax.broadcasted_iota(jnp.int32, (80, W), 0)
    col = lax.broadcasted_iota(jnp.int32, (80, W), 1)
    moved = jnp.zeros((36, W), F32)
    for ch in range(2):
        spot = jnp.where(2 * lane + ch == col, 1.0, 0.0)
        moved += jnp.dot(o_ref[ch, :36, :80], spot, precision=HI, preferred_element_type=F32)
    put_rows(s_ref, OUT, moved)
    b0 = jnp.where(c == 0, dbout[0:1, 0:1], dbout[2:3, 0:1])
    b1 = jnp.where(c == 0, dbout[1:2, 0:1], dbout[3:4, 0:1])
    at = lax.broadcasted_iota(jnp.int32, (1, W), 1)
    put_rows(s_ref, OUTB, jnp.where(at == 0, b0, jnp.where(at == 1, b1, 0.0)))
    s_ref[:, OUTB + 1 :, :] = jnp.zeros((2, 4 * R1 // 5 - OUTB - 1, 128), F32)
    by_owner(s_ref, flat, out1, R1)
    flow.ready(0)

    flow.need(15, 8, 10)
    conv_grads(a1, go_ref, s_ref, 39)
    n = normed_of(h0, 0)
    g = conv_back_rows(g_ref, w1) * silu_slope(n * vec0[1:2, :] + vec0[2:3, :])
    g, dgain, dbias = norm_back(g, n, 0, vec0[1:2, :])
    g = dh[...] + g
    cols = jnp.concatenate([shift_lanes(noisy[...], t) for t in range(9)], axis=0).astype(BF)
    put_rows(s_ref, 0, nn(cols, own(g).astype(BF)))
    for r, v in zip(VEC0, (colsum(g), dgain, dbias, total)):
        put_rows(s_ref, r, own(v))
    s_ref[:, 4 * FRONT // 5 : 4 * R0 // 5, :] = jnp.zeros((2, 4 * (R0 - FRONT) // 5, 128), F32)
    by_owner(s_ref, flat, out0, R0)


FIRST = (0, 0, 1, 2, 3)
SECOND = (0, 1, 2, 3, 3)


def time_rows(facts, count):
    row = lax.axis_index(DP) * count + lax.broadcasted_iota(jnp.int32, (count, 1), 0)

    def wide(at, n):
        return jnp.concatenate([facts[:, at + i, :] for i in range(n)], axis=1)

    def meets(u, k):
        spot = jnp.where(k == lax.broadcasted_iota(jnp.int32, (1, u.shape[1]), 1), 1.0, 0.0).astype(BF)
        return nt(spot, u.astype(BF))

    total = jnp.zeros((count, 128), F32)
    for u, at, start, size in ((wide(FE, 3)[:, :D], FD1, T1, D), (wide(FU1, 10), FD2, T2, 4 * D)):
        rel = row - start
        k, line = rel // 5, rel % 5
        met = meets(u, jnp.where(rel < 0, -1, k))
        for j in range(5):
            g = facts[:, at + j, :]
            total += nn(jnp.where(line == j, met, 0.0).astype(BF), g.astype(BF))
            total += jnp.where((rel >= 0) & (k == size) & (line == j), colsum(g), 0.0)
    rel = row - T3
    group, line = rel // 5, rel % 5
    d3 = wide(FD3, 2)[:, :W]
    zero = jnp.zeros((d3.shape[0], 128), F32)
    u = wide(FU2, 10)
    for picks, shift in ((FIRST, 0), (SECOND, 1)):
        k = jnp.full_like(rel, -1)
        for j in range(5):
            k = jnp.where((rel >= 0) & (line == j), 4 * group + picks[j], k)
        met = meets(u, k)
        for j in range(5):
            if shift == 0:
                lo = (0, 128, 96, 64, 32)[j]
                g = d3[:, lo : min(lo + 128, W)]
                g = jnp.concatenate([g, zero[:, : 128 - g.shape[1]]], axis=1) if g.shape[1] < 128 else g
            else:
                if j in (0, 4):
                    continue
                g = jnp.concatenate([zero[:, : 32 * j], d3[:, : 128 - 32 * j]], axis=1)
            total += nn(jnp.where(line == j, met, 0.0).astype(BF), g.astype(BF))
            total += jnp.where((k == 4 * D) & (line == j), colsum(g), 0.0)
    return total


def update_kernel(with_time, params, momentum, ema, sum1, sum0, facts, new_params, new_momentum, new_ema, sums):
    total = facts[0, FL : FL + 1, :]
    for i in range(1, facts.shape[0]):
        total += facts[i, FL : FL + 1, :]
    sums[...] = total
    scale = 1.0 / (LAT * jnp.maximum(total[:, 1:2], 1.0))
    first = sum0[...]
    if with_time:
        first += time_rows(facts, sum0.shape[0])
    for p, g in enumerate((first, sum1[...])):
        g = g * scale
        m = MU * momentum[p] + g
        new_momentum[p] = m
        w = params[p] - LR * (g + MU * m)
        new_params[p] = w
        new_ema[p] = ED * ema[p] + (1.0 - ED) * w


ROWS = 856
SLAB = 864
SOME = 240
REST = SLAB - 3 * SOME


def send(src, dst, sems, i, j, target):
    copy = pltpu.make_async_remote_copy(
        src_ref=src, dst_ref=dst, send_sem=sems[0].at[i], recv_sem=sems[1].at[j],
        device_id={DP: target}, device_id_type=pl.DeviceIdType.MESH,
    )
    copy.start()
    return copy


PIECES = tuple(slice(16 * a, 16 * b) for a, b in ((0, 7), (7, 14), (14, 21), (21, 28), (28, 35), (35, 42), (42, 48), (48, 54)))


def gather_kernel(
    params, step, latents, noise, g0, g1, e, noisy, vec, p1, p2, stats, w1b_out, tw2_out, tw3_out, h0_out, h1_out, a1_out,
    low, slabs, flat, s_ref, w1b, tw2, tw3, h0, h1, a1, w1, win, tv, half1, half2, half3, sh, acc,
    send_sem, recv_sem, keep_sem, slab_sem, out_sem, swap_sem,
):
    low[:, :ROWS, :] = params[...].astype(BF)
    low[:, ROWS:, :] = jnp.zeros((2, SLAB - ROWS, 128), BF)
    me, y = lax.axis_index(DP), lax.axis_index(CH)
    k, x, z = me % 2, (me // 2) % 2, me // 4
    core = {DP: me + 1 - 2 * k}
    side = {DP: me + 2 - 4 * x}
    other = {CH: 1 - y}
    ring = [{DP: (me + 4 * o) % 16} for o in range(4)]
    barrier = pltpu.get_barrier_semaphore()
    for target in [core, side, other] + ring[1:]:
        pl.semaphore_signal(barrier, inc=1, device_id=target, device_id_type=pl.DeviceIdType.MESH)
    pl.semaphore_wait(barrier, 6)
    count = [0]
    started = []

    def push(ref, target):
        i = count[0]
        count[0] += 1
        return [start(ref, ref, i, i, target)]

    def start(src, dst, i, j, target):
        copy = pltpu.make_async_remote_copy(
            src_ref=src, dst_ref=dst, send_sem=send_sem.at[i], recv_sem=recv_sem.at[j],
            device_id=target, device_id_type=pl.DeviceIdType.MESH,
        )
        copy.start()
        started.append(copy)
        return copy

    def push_ring(ref):
        i = count[0]
        count[0] += 3
        return [start(ref, ref, i + o - 1, i + 3 - o, ring[o]) for o in (2, 1, 3)]

    def arrive(copies):
        for copy in copies:
            copy.wait_recv()

    keeps = []
    for p, g in enumerate((g0, g1)):
        keep = pltpu.make_async_copy(low.at[p], g.at[y, z, x, k], keep_sem.at[p])
        keep.start()
        keeps.append(keep)
    work = [(p, g, rows, p * (i % 2)) for p, g in enumerate((g0, g1)) for i, rows in enumerate(PIECES)]
    first, second, third, last = {}, {}, {}, ([], [])

    def begin(i):
        p, g, rows, _ = work[i]
        if i % len(PIECES) == 0:
            keeps[p].wait()
        first[i] = push_ring(g.at[y, z, x, k, rows])

    def middle(i):
        p, g, rows, turn = work[i]
        arrive(first[i])
        second[i] = push(g.at[y, :, x, k, rows], other if turn else side)
        last[p].extend(push(g.at[y, :, x, k, rows], core))

    def finish(i):
        p, g, rows, turn = work[i]
        zs = slice(0, 4 if p else 2)
        arrive(second[i])
        if turn:
            third[i] = push(g.at[:, :, x, k, rows], side)
            last[p].extend(push(g.at[1 - y, :, x, k, rows], core))
        else:
            third[i] = push(g.at[y, zs, :, k, rows], other)
            last[p].extend(push(g.at[y, :, 1 - x, k, rows], core))

    def pass_on(i):
        p, g, rows, turn = work[i]
        zs = slice(0, 4 if p else 2)
        arrive(third[i])
        last[p].extend(push(g.at[:, :, 1 - x, k, rows] if turn else g.at[1 - y, zs, :, k, rows], core))

    outs = [
        pltpu.make_async_copy(src, dst, out_sem.at[i])
        for i, (src, dst) in enumerate(
            ((w1b, w1b_out), (tw2, tw2_out), (tw3, tw3_out), (h0, h0_out), (h1, h1_out), (a1, a1_out))
        )
    ]
    fetches = [
        pltpu.make_async_copy(g0.at[a, b], slabs.at[a, b], slab_sem.at[i])
        for i, (a, b) in enumerate([(y, b) for b in range(4)] + [(1 - y, b) for b in range(2)])
    ]
    slabs[1 - y, 2:4] = jnp.zeros((2,) + slabs.shape[2:], BF)

    def fetch():
        arrive(last[0])
        for copy in fetches:
            copy.start()

    def flat_half(a):
        if a == 0:
            for copy in fetches:
                copy.wait()
        for t in range(16):
            flat[a, t * ROWS : (t + 1) * ROWS, :] = slabs[a, t // 4, t // 2 % 2, t % 2, :ROWS, :].astype(F32)

    def front():
        take_front(s_ref, win, w1, w1b, vec)
        outs[0].start()

    def times():
        for i in range(4):
            tw2[i] = own(get_rows(s_ref, U2 + i, 4 * D, 4)).astype(BF)
        tw3[...] = own(get_rows(s_ref, U3, 4 * D)).astype(BF)
        outs[1].start()
        outs[2].start()

    def swap(i, ref):
        return pltpu.make_async_remote_copy(
            src_ref=ref.at[y], dst_ref=ref.at[y], send_sem=swap_sem.at[i], recv_sem=swap_sem.at[3 + i],
            device_id=other, device_id_type=pl.DeviceIdType.MESH,
        )

    def units(u, w, start, size):
        parts = [nn(u, w(i)) + own(get_rows(s_ref, start + 4 * size + i, 1)) for i in range(4)]
        return jnp.concatenate(parts, axis=1)

    swaps = [swap(0, half1), swap(1, half2), swap(2, half3)]

    def time_one():
        u = e[...].astype(BF)
        half1[y] = units(u, lambda i: own(get_rows(s_ref, U1 + i, D, 4)).astype(BF), U1, D)
        swaps[0].start()

    def time_two():
        swaps[0].wait_recv()
        p1[...] = jnp.concatenate([half1[0], half1[1]], axis=1)
        half2[y] = units(silu(p1[...]).astype(BF), lambda i: tw2[i], U2, 4 * D)
        swaps[1].start()

    def time_three():
        swaps[1].wait_recv()
        p2[...] = jnp.concatenate([half2[0], half2[1]], axis=1)
        half3[y] = nn(silu(p2[...]).astype(BF), tw3[...]) + own(get_rows(s_ref, U3 + 4 * D, 1))
        swaps[2].start()

    def time_last():
        swaps[2].wait_recv()
        tv[...] = jnp.concatenate([half3[0], half3[1]], axis=1)[:1]

    def both(*steps):
        def one():
            for step in steps:
                step()

        return one

    opening, *rows_of_taps = start_steps(noisy, tv, win, w1, vec, h0, h1, a1, stats, sh, acc)
    todo = [
        fetch,
        lambda: flat_half(0),
        lambda: flat_half(1),
        lambda: unroll(flat, s_ref, 0, 9),
        lambda: unroll(flat, s_ref, 9, 18),
        lambda: unroll(flat, s_ref, 18, 27),
        lambda: unroll(flat, s_ref, 27, R1 // 400),
        time_one,
        both(front, times),
        time_two,
        opening,
        both(outs[3].start, outs[5].start, rows_of_taps[0]),
        time_three,
        rows_of_taps[1],
        time_last,
        both(rows_of_taps[2], outs[4].start),
    ]
    ahead = 4
    for i in range(ahead):
        begin(i)
    e[...] = jnp.broadcast_to(time_features(step[...]), (8, D))
    add_noise(step[...], latents, noise, noisy)
    for i in range(len(work) + 2):
        if i < len(work):
            middle(i)
            if i + ahead < len(work):
                begin(i + ahead)
        if i - 3 >= len(PIECES) and todo:
            todo.pop(0)()
        if 0 <= i - 1 < len(work):
            finish(i - 1)
        if 0 <= i - 3 < len(work):
            pass_on(i - 3)
        if i - 3 >= len(PIECES) - 1 and todo:
            todo.pop(0)()
    pass_on(len(work) - 1)
    for step in todo:
        step()
    for copy in outs:
        copy.wait()
    for copy in swaps:
        copy.wait_send()
    arrive(last[1])
    for copy in started:
        copy.wait_send()


def gather_weights(*operands):
    hbm, vm = pl.BlockSpec(memory_space=pl.ANY), pl.BlockSpec(memory_space=pltpu.VMEM)
    gathered = sds((2, 4, 2, 2, SLAB, 128), BF)
    large = (sds((3, D, 3 * D), BF), sds((4, 4 * D, W), BF), sds((4 * D, W), BF))
    large += (sds((N, D)), sds((N, D)), sds((N, D), BF))
    small = (sds((8, D)), sds((LAT, N)), sds((8, D)), sds((8, 4 * D)), sds((8, 4 * D)), sds((8, D)))
    dma = pltpu.SemaphoreType.DMA
    return pl.pallas_call(
        gather_kernel,
        out_shape=(gathered, gathered) + small + large,
        in_specs=[vm] * 4,
        out_specs=(hbm, hbm) + (vm,) * len(small) + (hbm,) * len(large),
        scratch_shapes=[
            pltpu.VMEM((2, SLAB, 128), BF),
            pltpu.VMEM(gathered.shape, BF),
            pltpu.VMEM((2, 16 * ROWS, 128), F32),
            pltpu.VMEM((3, 4 * R1 // 5, 128), F32),
            *(pltpu.VMEM(v.shape, v.dtype) for v in large),
            pltpu.VMEM((3, 3 * D, D), BF),
            pltpu.VMEM((36, D), BF),
            pltpu.VMEM((1, D), F32),
            pltpu.VMEM((2, 8, 2 * D), F32),
            pltpu.VMEM((2, 8, 2 * D), F32),
            pltpu.VMEM((2, 8, W), F32),
            pltpu.VMEM((N + 2 * SIDE, 3 * D), BF),
            pltpu.VMEM((8, D), F32),
            dma((128,)),
            dma((128,)),
            dma((2,)),
            dma((6,)),
            dma((6,)),
            dma((6,)),
        ],
        compiler_params=pltpu.CompilerParams(collective_id=2, has_side_effects=True, vmem_limit_bytes=63 * 2**20),
    )(*operands)


def add_up(*terms):
    total = terms[0].astype(F32)
    for term in terms[1:]:
        total += term.astype(F32)
    return total


def reduce_kernel(
    p1, p0, dtv, tw2_in, tw3_in, p1t, p2t, e, mask, loss, sum1, sum0, all_facts,
    kp1, kp0, tw2, tw3, facts, r1, sa, rx, ta, rz, r1b, sb, rbz, tb, rbx, some, land, fx, timed, send_sem, recv_sem, fsend, frecv, gsend, grecv, lsem, half, ssem,
):
    me = lax.axis_index(DP)
    k, x, z = me % 2, (me // 2) % 2, me // 4
    kept = [
        pltpu.make_async_copy(src, dst, lsem.at[i])
        for i, (src, dst) in enumerate(((p1.at[k], kp1), (p0.at[k], kp0), (tw2_in, tw2), (tw3_in, tw3)))
    ]
    for copy in kept:
        copy.start()
    barrier = pltpu.get_barrier_semaphore()
    for o in range(1, 16):
        pl.semaphore_signal(barrier, inc=1, device_id={DP: (me + o) % 16}, device_id_type=pl.DeviceIdType.MESH)
    y = lax.axis_index(CH)
    pl.semaphore_signal(barrier, inc=1, device_id={CH: 1 - y}, device_id_type=pl.DeviceIdType.MESH)
    pl.semaphore_wait(barrier, 16)
    sems = (send_sem, recv_sem)

    def swap(i):
        copy = pltpu.make_async_remote_copy(
            src_ref=half.at[i, y], dst_ref=half.at[i, y], send_sem=ssem.at[i], recv_sem=ssem.at[2 + i],
            device_id={CH: 1 - y}, device_id_type=pl.DeviceIdType.MESH,
        )
        copy.start()
        return copy

    core = me + 1 - 2 * k
    side = me + 2 - 4 * x
    chunks = [p0] + [p1.at[:, :, SOME * i : SOME * (i + 1)] for i in range(3)]
    mine = [kp0] + [kp1.at[:, SOME * i : SOME * (i + 1)] for i in range(3)]
    rest = p1.at[:, :, 3 * SOME :]

    def over_z(src, dst, base):
        return [
            send(src.at[(z + o) % 4], dst.at[3 - o], sems, base + o - 1, base + 3 - o, (me + 4 * o) % 16)
            for o in (2, 1, 3)
        ]

    over_core_b = send(rest.at[1 - k], r1b, sems, 20, 20, core)
    over_core = [send(ref.at[1 - k], r1.at[i], sems, i, i, core) for i, ref in enumerate(chunks)]
    for copy in kept:
        copy.wait()
    half[0, y] = nt(jnp.broadcast_to(own(dtv[...]), (8, W)).astype(BF), tw3[...])
    swaps = [swap(0)]
    over_core_b.wait_recv()
    for m in range(8):
        sb[m // 2, m % 2] = add_up(kp1[m, 3 * SOME :], r1b[m]).astype(BF)
    over_z_b = over_z(sb, rbz, 21)
    over_x = []
    for i, ref in enumerate(mine):
        over_core[i].wait_recv()
        for m in range(8):
            sa[i, m % 2, m // 2] = add_up(ref[m], r1[i, m]).astype(BF)
        over_x.append(send(sa.at[i, 1 - x], rx.at[i], sems, 4 + i, 4 + i, side))
        if i == 1:
            swaps[0].wait_recv()
            d2 = (half[0, 0] + half[0, 1]) * silu_slope(p2t[...])
            mine2 = jnp.where(y == 0, d2[:, : 2 * D], d2[:, 2 * D :]).astype(BF)
            half[1, y] = sum(nt(mine2[:, W * j : W * (j + 1)], tw2[j]) for j in range(4))
            swaps.append(swap(1))
    swaps[1].wait_recv()
    d1 = (half[1, 0] + half[1, 1]) * silu_slope(p1t[...])
    put_facts(facts, e, p1t, p2t, d1, d2, dtv, mask, loss)
    fsems = (fsend, frecv)
    fx[z, x, k] = facts[...]
    facts_z = [send(facts, fx.at[z, x, k], fsems, o - 1, 3 - o, (me + 4 * o) % 16) for o in (2, 1, 3)]
    along = []
    for i in range(4):
        over_x[i].wait_recv()
        for m in range(4):
            ta[i, m] = add_up(sa[i, x, m], rx[i, m]).astype(BF)
        along.append(over_z(ta.at[i], rz.at[i], 8 + 3 * i))
        if i == 1:
            for copy in facts_z:
                copy.wait_recv()
            facts_x = send(fx.at[:, x, k], fx.at[:, x, k], fsems, 3, 3, side)
        if i == 3:
            facts_x.wait_recv()
            facts_core = send(fx.at[:, :, k], fx.at[:, :, k], fsems, 4, 4, core)
    for copy in over_z_b:
        copy.wait_recv()
    for m in range(2):
        tb[m] = add_up(sb[z, m], rbz[0, m], rbz[1, m], rbz[2, m]).astype(BF)
    over_x_b = send(tb.at[1 - x], rbx, sems, 24, 24, side)

    def done(i):
        for copy in along[i]:
            copy.wait_recv()
        return add_up(ta[i, z], rz[i, 0], rz[i, 1], rz[i, 2])

    facts_core.wait_recv()
    all_facts[...] = fx[...].reshape(16, FACTS, 128)
    timed[...] = time_rows(all_facts, ROWS)
    some[...] = done(0)

    @pl.when(me > 0)
    def _():
        @pl.loop(0, SOME // 8)
        def _(g):
            row = SOME * me + 8 * g
            owner = row // ROWS
            at = pl.multiple_of(row - ROWS * owner, 8)
            pltpu.make_async_remote_copy(
                src_ref=some.at[pl.ds(pl.multiple_of(8 * g, 8), 8)], dst_ref=land.at[pl.ds(at, 8)],
                send_sem=gsend, recv_sem=grecv, device_id={DP: owner}, device_id_type=pl.DeviceIdType.MESH,
            ).start()

    for i in range(3):
        sum1[SOME * i : SOME * (i + 1), :] = done(i + 1)
    over_x_b.wait_recv()
    sum1[3 * SOME :, :] = add_up(tb[x, : ROWS - 3 * SOME], rbx[: ROWS - 3 * SOME])

    def landed(lo, hi):
        part = land.at[lo:hi]
        pltpu.make_async_remote_copy(
            src_ref=part, dst_ref=part, send_sem=gsend, recv_sem=grecv,
            device_id={DP: me}, device_id_type=pl.DeviceIdType.MESH,
        ).wait_recv()
        sum0[lo:hi, :] = land[lo:hi, :] + timed[lo:hi, :]

    @pl.when(me == 0)
    def _():
        landed(SOME, ROWS)
        sum0[:SOME, :] = some[...] + timed[:SOME, :]

    @pl.when((me > 0) & (me < 4))
    def _():
        landed(0, ROWS)

    @pl.when(me == 4)
    def _():
        landed(0, 16 * SOME - 4 * ROWS)
        sum0[16 * SOME - 4 * ROWS :, :] = timed[16 * SOME - 4 * ROWS :, :]

    @pl.when(me > 4)
    def _():
        sum0[...] = timed[...]

    @pl.when(me > 0)
    def _():
        pltpu.make_async_remote_copy(
            src_ref=some, dst_ref=some, send_sem=gsend, recv_sem=grecv,
            device_id={DP: me}, device_id_type=pl.DeviceIdType.MESH,
        ).wait_send()

    for copy in [over_core_b, over_x_b] + over_core + over_z_b + over_x + sum(along, []) + facts_z + [facts_x, facts_core] + swaps:
        copy.wait_send()


def sum_over_samples(*operands):
    vm, hbm = pl.BlockSpec(memory_space=pltpu.VMEM), pl.BlockSpec(memory_space=pl.ANY)
    dma = pltpu.SemaphoreType.DMA
    return pl.pallas_call(
        reduce_kernel,
        out_shape=(sds((ROWS, 128)), sds((ROWS, 128)), sds((16, FACTS, 128))),
        in_specs=[hbm, hbm, vm, hbm, hbm] + [vm] * 5,
        out_specs=(vm,) * 3,
        scratch_shapes=[
            pltpu.VMEM((8, SLAB, 128), BF),
            pltpu.VMEM((8, SOME, 128), BF),
            pltpu.VMEM((4, 4 * D, W), BF),
            pltpu.VMEM((4 * D, W), BF),
            pltpu.VMEM((FACTS, 128), F32),
            pltpu.VMEM((4, 8, SOME, 128), BF),
            pltpu.VMEM((4, 2, 4, SOME, 128), BF),
            pltpu.VMEM((4, 4, SOME, 128), BF),
            pltpu.VMEM((4, 4, SOME, 128), BF),
            pltpu.VMEM((4, 3, SOME, 128), BF),
            pltpu.VMEM((8, REST, 128), BF),
            pltpu.VMEM((4, 2, REST, 128), BF),
            pltpu.VMEM((3, 2, REST, 128), BF),
            pltpu.VMEM((2, REST, 128), BF),
            pltpu.VMEM((REST, 128), BF),
            pltpu.VMEM((SOME, 128), F32),
            pltpu.VMEM((ROWS, 128), F32),
            pltpu.VMEM((4, 2, 2, FACTS, 128), F32),
            pltpu.VMEM((ROWS, 128), F32),
            dma((25,)),
            dma((25,)),
            dma((5,)),
            dma((5,)),
            dma,
            dma,
            dma((4,)),
            pltpu.VMEM((2, 2, 8, 4 * D), F32),
            dma((4,)),
        ],
        compiler_params=pltpu.CompilerParams(
            collective_id=1, has_side_effects=True, vmem_limit_bytes=62 * 2**20
        ),
    )(*operands)


def time_features(steps):
    ladder = lax.broadcasted_iota(jnp.int32, (1, D // 2), 1).astype(F32)
    angles = steps.astype(F32) * jnp.exp(-math.log(10000.0) * ladder / (D // 2))
    return jnp.concatenate([jnp.cos(angles), jnp.sin(angles)], axis=1)


def add_noise(step, latents, noise, noisy):
    shape = (8, 128)
    level = 128 * lax.broadcasted_iota(jnp.int32, shape, 0) + lax.broadcasted_iota(jnp.int32, shape, 1)
    lowest, highest = 0.00085**0.5, 0.012**0.5
    beta = jnp.square(lowest + (highest - lowest) * level.astype(F32) / 999.0)
    logs = jnp.where(level <= step, jnp.log(1.0 - beta), 0.0)
    abar = jnp.exp(jnp.sum(jnp.sum(logs, axis=1, keepdims=True), axis=0, keepdims=True))
    noisy[...] = jnp.sqrt(abar) * latents[...] + jnp.sqrt(1.0 - abar) * noise[...]


def prepare_kernel(step, latents, noise, e, noisy):
    e[...] = jnp.broadcast_to(time_features(step[...]), (8, D))
    add_noise(step[...], latents, noise, noisy)


def shards(params, momentum, ema_params, latents, noise_eps, timesteps, pixel_mask, context):
    c = lax.axis_index(CH)
    d = lax.axis_index(DP)
    n_dp = lax.axis_size(DP)
    rows_dev = params.shape[2]
    rows_all = rows_dev * n_dp
    quick = n_dp == 16 and rows_dev == ROWS
    step, noise = timesteps[:, None], noise_eps[0]
    if quick:
        _, part1, e, noisy, vec0, p1, p2, stats, w1b, tw2, tw3, h0, h1, a1 = gather_weights(
            params[0], step, latents[0], noise
        )
        part1 = part1.reshape(2, 16, SLAB, 128)
    else:
        e, noisy = kcall(prepare_kernel, (sds((8, D)), sds((LAT, N))), (step, latents[0], noise))
        low = params[0].astype(BF)
        part0, part1 = (lax.all_gather(lax.all_gather(low[i], CH, axis=0), DP, axis=1) for i in range(2))

    px = (N, D)
    hx = (HEADS, N, HD)
    sh = (N + 2 * SIDE, 3 * D)
    taps, back = sds((3, 3 * D, D), BF), sds((3, D, 3 * D), BF)
    flat = pltpu.VMEM((2, rows_all, 128), F32)
    unrolled = pltpu.VMEM((3, 4 * R1 // 5, 128), F32)
    units = sds((8, 4 * D))
    if not quick:
        win, w1, w1b, vec0, tw2, tw3, tv, p1, p2 = kcall(
            partial(unpack0_kernel, rows_dev),
            (sds((36, D), BF), taps, back, sds((8, D)), sds((4, 4 * D, D), BF), sds((4 * D, D), BF), sds((1, D)))
            + (units, units),
            (part0, e),
            (flat, unrolled),
        )
        h0, h1, a1, stats = kcall(
            start_kernel,
            (sds(px), sds(px), sds(px, BF), sds((8, D))),
            (noisy, tv, win, w1, vec0),
            (pltpu.VMEM(sh, BF), pltpu.VMEM((8, D), F32)),
        )
    c2, c2b, tr, mats, kvw, vec1, gib, wout, outb = kcall(
        partial(unpack1_kernel, rows_dev),
        (taps, back, sds((4, D, D), BF), sds((16, D, D), BF), sds((2, CTX, D), BF))
        + (sds((24, D)), sds((8, D)), sds((36, D), BF), sds((1, D))),
        (part1,),
        (flat, unrolled, pltpu.VMEM((2, 40, 128), F32)),
    )
    h2, z0, a2, ntr, x1, q, k, v, stats = kcall(
        front_kernel,
        (sds(px),) * 2 + (sds(px, BF),) * 3 + (sds(hx, BF),) * 3 + (sds((8, D)),),
        (h0, h1, stats, c2, tr, vec1),
        (pltpu.VMEM(sh, BF), pltpu.VMEM((8, D), F32)),
        late=(0, 3, 4),
        early=range(8),
    )
    o, lse = kcall(
        attend_kernel, (sds(px, BF), sds((HEADS, 1, N))), (q, k, v), (pltpu.VMEM((D, N), F32),)
    )
    square = (D, W)
    dz1, dh3, dos, loss, gd, ggi, ggo, gkv, dvec, dgib, dwout, dbout = kcall(
        middle_kernel,
        (sds(px), sds(px), sds(hx, BF), sds((1, 1)))
        + (sds((4,) + square, BF), sds((8,) + square, BF), sds((4,) + square, BF), sds((2, CTX, W), BF))
        + (sds((24, D)), sds((8, D)), sds((36, D)), sds((8, 128))),
        (o, z0, h2, context[0], noise, pixel_mask, mats, kvw, vec1, gib, wout, outb),
        [pltpu.VMEM(px, F32)] * 3
        + [pltpu.VMEM(px, BF)] * 4
        + [
            pltpu.VMEM((4, N, D), BF),
            pltpu.VMEM((4, N, D), F32),
            pltpu.VMEM((4, N, D), F32),
            pltpu.VMEM(px, BF),
            pltpu.VMEM(px, BF),
            pltpu.VMEM((HEADS * KEYS, D), BF),
            pltpu.VMEM((HEADS * KEYS, D), BF),
            pltpu.VMEM((N, HEADS * KEYS), F32),
            pltpu.VMEM((N, HEADS * KEYS), BF),
            pltpu.VMEM((8, D), F32),
            pltpu.VMEM((36, N), F32),
        ]
        + [pltpu.VMEM((D, N), BF)] * 4,
        late=(7, 6, 1, 2),
        early=(0, 1, 2, 4, 5, 6, 7),
    )
    dq, dk, dv = kcall(
        attend_back_kernel,
        (sds(px, BF),) * 3,
        (q, k, v, dos, lse),
        (pltpu.VMEM((D, N), F32), pltpu.VMEM(hx, F32), pltpu.VMEM(hx, F32)),
    )
    front = -(-FRONT // (16 * n_dp)) * 16 * n_dp
    lead = (2, 8) if quick else (n_dp,)
    own1, own0, dtv = kcall(
        back_kernel,
        (
            sds(lead + (SLAB if quick else rows_dev, 128), BF),
            sds(lead + (front // n_dp, 128), BF),
            sds((1, D)),
        ),
        (dq, dk, dv, dz1, dh3, z0, h2, h1, h0, stats, w1b, c2b, tr, vec0, vec1, a1, a2, ntr, x1, noisy,
         gd, ggi, ggo, gkv, dvec, dgib, dwout, dbout),
        (
            pltpu.VMEM(px, F32),
            pltpu.VMEM(sh, BF),
            pltpu.VMEM((sh[0], 3 * W), BF),
            pltpu.VMEM((24, D), F32),
            pltpu.VMEM((2, 4 * R1 // 5, 128), F32),
            pltpu.VMEM((7600, 128), F32),
            pltpu.VMEM((2, 40, 128), F32),
        ),
        late=(5, 3, 17, 6, 4, 16, 7, 11, 20, 21, 22, 23, 15, 8, 10),
        early=(0,),
    )
    timed = (dtv, tw2, tw3, p1, p2, e, pixel_mask, loss)
    if quick:
        sum1, sum0, all_facts = sum_over_samples(own1, own0, *timed)
    else:
        facts = kcall(time_back, sds((FACTS, 128)), timed)
        sum1 = lax.psum_scatter(own1, DP, scatter_dimension=0).astype(F32)
        sum0 = lax.all_gather(lax.psum_scatter(own0, DP, scatter_dimension=0), DP, axis=0, tiled=True)
        sum0 = jnp.pad(sum0, ((0, rows_all - front), (0, 0)))
        sum0 = lax.dynamic_slice_in_dim(sum0, d * rows_dev, rows_dev, 0).astype(F32)
        all_facts = lax.all_gather(facts, DP, axis=0)
    state = sds((2, rows_dev, 128))
    new_params, new_momentum, new_ema, sums = kcall(
        partial(update_kernel, not quick),
        (state, state, state, sds((1, 128))),
        (params[0], momentum[0], ema_params[0], sum1, sum0, all_facts),
    )
    return (new_params[None], new_momentum[None], new_ema[None], sums[0, 0], sums[0, 1])


def solution(mesh):
    packed = P(CH, None, DP, None)
    row = P(DP, None, None)
    return jax.shard_map(
        shards,
        mesh=mesh,
        in_specs=(packed, packed, packed, row, row, P(DP), P(DP, None), row),
        out_specs=(packed, packed, packed, P(), P()),
        check_vma=False,
    )
```

profile of v0, /device:TPU:1, one launch (start us, length us, event | category | flops | bytes accessed | tf_op | source)
XLA Modules:
  0.0 288.0 jit_solution(5982637722399094815)
XLA Ops:
  1.3 77.8 %shard_map.119 = (bf16[2,4,2,2,864,128]{5,4,3,2,1,0:T(8,128)(2,1)}, bf16[2,4,2,2,864,128]{5,4,3,2,1,0:T(8,128)(2,1)}, f32[8,320]{1,0:T(8,128)}, f32[4,1024]{1,0:...) custom-call(f32[2,856,128]{2,1,0:T(8,128)} %bitcast.15, ...), custom_call_target="tpu_custom_call" | custom-call | tf_op jit(solution)/shard_map/pallas_call | solution.py:1114
  79.1 15.1 %shard_map.120 = (bf16[3,960,320]{2,1,0:T(8,128)(2,1)}, bf16[3,320,960]{2,1,0:T(8,128)(2,1)}, bf16[4,320,320]{2,1,0:T(8,128)(2,1)}, bf16[16,320,320]{2,1,0:T(8,1...) custom-call(bf16[2,16,864,128]{3,2,1,0:T(8,128)(2,1)} %bitcast.14), custom_call_target="tpu_custom_call" | custom-call | tf_op jit(solution)/shard_map/pallas_call | solution.py:112
  94.2 14.6 %shard_map.121 = (f32[1024,320]{1,0:T(8,128)}, f32[1024,320]{1,0:T(8,128)}, bf16[1024,320]{1,0:T(8,128)(2,1)}, bf16[1024,320]{1,0:T(8,128)(2,1)}, bf16[1024,320]...) custom-call(f32[1024,320]{1,0:T(8,128)} %get-tuple-element.63.refs_0, ...), custom_call_target="tpu_custom_call" | custom-call | tf_op jit(solution)/shard_map/pallas_call | solution.py:112
  108.8 16.3 %shard_map.122 = (bf16[1024,320]{1,0:T(8,128)(2,1)}, f32[8,1,1024]{2,1,0:T(1,128)}) custom-call(bf16[8,1024,40]{2,1,0:T(8,128)(2,1)} %get-tuple-element.70.refs_0_, bf16[8,1024,40]{2,1,0:T(8,128)(2,1)} %get-tuple-element.71.refs_1_, bf16[8,1024,40]{2,1,0:T(8,128)(2,1)} %get-tuple-element.72.refs_2_), custom_call_target="tpu_custom_call" | custom-call | tf_op jit(solution)/shard_map/pallas_call | solution.py:112
  125.1 45.0 %shard_map.123 = (f32[1024,320]{1,0:T(8,128)}, f32[1024,320]{1,0:T(8,128)}, bf16[8,1024,40]{2,1,0:T(8,128)(2,1)}, f32[1,1]{1,0:T(1,128)}, bf16[4,320,160]{2,1,0:...) custom-call(bf16[1024,320]{1,0:T(8,128)(2,1)} %get-tuple-element.73., ...), custom_call_target="tpu_custom_call" | custom-call | tf_op jit(solution)/shard_map/pallas_call | solution.py:112
  170.2 29.8 %shard_map.124 = (bf16[1024,320]{1,0:T(8,128)(2,1)}, bf16[1024,320]{1,0:T(8,128)(2,1)}, bf16[1024,320]{1,0:T(8,128)(2,1)}) custom-call(bf16[8,1024,40]{2,1,0:T(8,128)(2,1)} %get-tuple-element.70.refs_0_, bf16[8,1024,40]{2,1,0:T(8,128)(2,1)} %get-tuple-element.71.refs_1_, bf16[8,1024,40]{2,1,0:T(8,128)(2,1)} %get-tuple-element.72.refs_2_, ...), custom_call_target="tpu_custom_call" | custom-call | tf_op jit(solution)/shard_map/pallas_call | solution.py:112
  199.9 32.9 %shard_map.125 = (bf16[2,8,864,128]{3,2,1,0:T(8,128)(2,1)}, bf16[2,8,240,128]{3,2,1,0:T(8,128)(2,1)}, f32[1,320]{1,0:T(1,128)}) custom-call(bf16[1024,320]{1,0:T(8,128)(2,1)} %get-tuple-element.83.refs_0_, bf16[1024,320]{1,0:T(8,128)(2,1)} %get-tuple-element.84.refs_1_, bf16[1024,320]{1,0:T(8,128)(2,1)} %get-tuple-element.85.refs_2_, ...), custom_call_target="tpu_custom_call" | custom-call | tf_op jit(solution)/shard_map/pallas_call | solution.py:112
  232.9 49.7 %shard_map.126 = (f32[856,128]{1,0:T(8,128)}, f32[856,128]{1,0:T(8,128)}, f32[16,40,128]{2,1,0:T(8,128)}) custom-call(bf16[2,8,864,128]{3,2,1,0:T(8,128)(2,1)} %get-tuple-element.105.p1, bf16[2,8,240,128]{3,2,1,0:T(8,128)(2,1)} %get-tuple-element.106.p0, f32[1,320]{1,0:T(1,128)} %get-tuple-element.107.dtv, bf16[4,1280,160]{2,1,0:T(8,128)(2,1)} %get-tuple-element.108.tw2_in, ...), custom_call_target="tpu_custom_call" | custom-call | tf_op jit(solution)/shard_map/pallas_call | solution.py:1305
  282.6 3.8 %shard_map.127 = (f32[2,856,128]{2,1,0:T(8,128)}, f32[2,856,128]{2,1,0:T(8,128)}, f32[2,856,128]{2,1,0:T(8,128)}, f32[1,128]{1,0:T(1,128)}) custom-call(f32[2,856,128]{2,1,0:T(8,128)} %bitcast.16, f32[2,856,128]{2,1,0:T(8,128)} %bitcast.17, f32[2,856,128]{2,1,0:T(8,128)} %bitcast.18, f32[856,128]{1,0:T(8,128)} %get-tuple-element.114.refs_3_, ...), custom_call_target="tpu_custom_call" | custom-call | tf_op jit(solution)/shard_map/pallas_call | solution.py:112
  286.5 1.3 fusion
where the time goes:
time: 291 us; the launch traced here: 288 us
  Pallas kernels  285 us (98%)
    pallas_call x7, Pallas kernels, kcall(): pl.pallas_call(whole, out_shape=outs, in_specs=[hbm if i in late else vm...  158 us
    pallas_call x1, Pallas kernels, gather_weights(): pl.pallas_call(gather_kernel, out_shape=(gathered, gathered) + small + la...  77.8 us
    pallas_call x1, Pallas kernels, sum_over_samples(): pl.pallas_call(reduce_kernel, out_shape=(sds((ROWS, 128)), sds((ROWS, 128...  49.7 us

commit v1 on v0

--- a/solution.py
+++ b/solution.py
@@ -864,11 +864,12 @@
     return total
 
 
-def update_kernel(with_time, params, momentum, ema, sum1, sum0, facts, new_params, new_momentum, new_ema, sums):
+def update_kernel(with_time, params, momentum, ema, sum1, sum0, facts, new_params, new_momentum, new_ema, loss, pixels):
     total = facts[0, FL : FL + 1, :]
     for i in range(1, facts.shape[0]):
         total += facts[i, FL : FL + 1, :]
-    sums[...] = total
+    loss[...] = total[:, 0:1]
+    pixels[...] = total[:, 1:2]
     scale = 1.0 / (LAT * jnp.maximum(total[:, 1:2], 1.0))
     first = sum0[...]
     if with_time:
@@ -1190,10 +1191,8 @@
 
     over_core_b = send(rest.at[1 - k], r1b, sems, 20, 20, core)
     over_core = [send(ref.at[1 - k], r1.at[i], sems, i, i, core) for i, ref in enumerate(chunks)]
-    for copy in kept:
-        copy.wait()
-    half[0, y] = nt(jnp.broadcast_to(own(dtv[...]), (8, W)).astype(BF), tw3[...])
-    swaps = [swap(0)]
+    kept[0].wait()
+    kept[1].wait()
     over_core_b.wait_recv()
     for m in range(8):
         sb[m // 2, m % 2] = add_up(kp1[m, 3 * SOME :], r1b[m]).astype(BF)
@@ -1204,7 +1203,12 @@
         for m in range(8):
             sa[i, m % 2, m // 2] = add_up(ref[m], r1[i, m]).astype(BF)
         over_x.append(send(sa.at[i, 1 - x], rx.at[i], sems, 4 + i, 4 + i, side))
-        if i == 1:
+        if i == 0:
+            kept[2].wait()
+            kept[3].wait()
+            half[0, y] = nt(jnp.broadcast_to(own(dtv[...]), (8, W)).astype(BF), tw3[...])
+            swaps = [swap(0)]
+        if i == 2:
             swaps[0].wait_recv()
             d2 = (half[0, 0] + half[0, 1]) * silu_slope(p2t[...])
             mine2 = jnp.where(y == 0, d2[:, : 2 * D], d2[:, 2 * D :]).astype(BF)
@@ -1240,9 +1244,6 @@
             copy.wait_recv()
         return add_up(ta[i, z], rz[i, 0], rz[i, 1], rz[i, 2])
 
-    facts_core.wait_recv()
-    all_facts[...] = fx[...].reshape(16, FACTS, 128)
-    timed[...] = time_rows(all_facts, ROWS)
     some[...] = done(0)
 
     @pl.when(me > 0)
@@ -1257,6 +1258,9 @@
                 send_sem=gsend, recv_sem=grecv, device_id={DP: owner}, device_id_type=pl.DeviceIdType.MESH,
             ).start()
 
+    facts_core.wait_recv()
+    all_facts[...] = fx[...].reshape(16, FACTS, 128)
+    timed[...] = time_rows(all_facts, ROWS)
     for i in range(3):
         sum1[SOME * i : SOME * (i + 1), :] = done(i + 1)
     over_x_b.wait_recv()
@@ -1487,12 +1491,12 @@
         sum0 = lax.dynamic_slice_in_dim(sum0, d * rows_dev, rows_dev, 0).astype(F32)
         all_facts = lax.all_gather(facts, DP, axis=0)
     state = sds((2, rows_dev, 128))
-    new_params, new_momentum, new_ema, sums = kcall(
+    new_params, new_momentum, new_ema, loss, pixels = kcall(
         partial(update_kernel, not quick),
-        (state, state, state, sds((1, 128))),
+        (state, state, state, sds((1, 1)), sds((1, 1))),
         (params[0], momentum[0], ema_params[0], sum1, sum0, all_facts),
     )
-    return (new_params[None], new_momentum[None], new_ema[None], sums[0, 0], sums[0, 1])
+    return (new_params[None], new_momentum[None], new_ema[None], loss.reshape(()), pixels.reshape(()))
 
 
 def solution(mesh):

time: 291 us -> 285 us (0.979)
  Pallas kernels: 285 us -> 279 us
    pallas_call x1, Pallas kernels: 49.7 us -> 43.6 us  [sum_over_samples(): pl.pallas_call(reduce_kernel, out_shape=(sds((ROWS, 128)), sds((ROWS, 128...]
where the time goes in v1:
time: 285 us; the launch traced here: 280 us
  Pallas kernels  279 us (98%)
    pallas_call x7, Pallas kernels, kcall(): pl.pallas_call(whole, out_shape=outs, in_specs=[hbm if i in late else vm...  158 us
    pallas_call x1, Pallas kernels, gather_weights(): pl.pallas_call(gather_kernel, out_shape=(gathered, gathered) + small + la...  77.7 us
    pallas_call x1, Pallas kernels, sum_over_samples(): pl.pallas_call(reduce_kernel, out_shape=(sds((ROWS, 128)), sds((ROWS, 128...  43.6 us

profile of v1, /device:TPU:1, one launch (start us, length us, event | category | flops | bytes accessed | tf_op | source)
XLA Modules:
  0.0 280.4 jit_solution(10337059834001807301)
XLA Ops:
  1.3 77.7 %shard_map.119 = (bf16[2,4,2,2,864,128]{5,4,3,2,1,0:T(8,128)(2,1)}, bf16[2,4,2,2,864,128]{5,4,3,2,1,0:T(8,128)(2,1)}, f32[8,320]{1,0:T(8,128)}, f32[4,1024]{1,0:...) custom-call(f32[2,856,128]{2,1,0:T(8,128)} %bitcast.15, ...), custom_call_target="tpu_custom_call" | custom-call | tf_op jit(solution)/shard_map/pallas_call | solution.py:1115
  79.0 15.1 %shard_map.120 = (bf16[3,960,320]{2,1,0:T(8,128)(2,1)}, bf16[3,320,960]{2,1,0:T(8,128)(2,1)}, bf16[4,320,320]{2,1,0:T(8,128)(2,1)}, bf16[16,320,320]{2,1,0:T(8,1...) custom-call(bf16[2,16,864,128]{3,2,1,0:T(8,128)(2,1)} %bitcast.14), custom_call_target="tpu_custom_call" | custom-call | tf_op jit(solution)/shard_map/pallas_call | solution.py:112
  94.1 14.6 %shard_map.121 = (f32[1024,320]{1,0:T(8,128)}, f32[1024,320]{1,0:T(8,128)}, bf16[1024,320]{1,0:T(8,128)(2,1)}, bf16[1024,320]{1,0:T(8,128)(2,1)}, bf16[1024,320]...) custom-call(f32[1024,320]{1,0:T(8,128)} %get-tuple-element.64.refs_0, ...), custom_call_target="tpu_custom_call" | custom-call | tf_op jit(solution)/shard_map/pallas_call | solution.py:112
  108.7 16.3 %shard_map.122 = (bf16[1024,320]{1,0:T(8,128)(2,1)}, f32[8,1,1024]{2,1,0:T(1,128)}) custom-call(bf16[8,1024,40]{2,1,0:T(8,128)(2,1)} %get-tuple-element.71.refs_0_, bf16[8,1024,40]{2,1,0:T(8,128)(2,1)} %get-tuple-element.72.refs_1_, bf16[8,1024,40]{2,1,0:T(8,128)(2,1)} %get-tuple-element.73.refs_2_), custom_call_target="tpu_custom_call" | custom-call | tf_op jit(solution)/shard_map/pallas_call | solution.py:112
  125.0 45.0 %shard_map.123 = (f32[1024,320]{1,0:T(8,128)}, f32[1024,320]{1,0:T(8,128)}, bf16[8,1024,40]{2,1,0:T(8,128)(2,1)}, f32[1,1]{1,0:T(1,128)}, bf16[4,320,160]{2,1,0:...) custom-call(bf16[1024,320]{1,0:T(8,128)(2,1)} %get-tuple-element.74., ...), custom_call_target="tpu_custom_call" | custom-call | tf_op jit(solution)/shard_map/pallas_call | solution.py:112
  170.1 29.8 %shard_map.124 = (bf16[1024,320]{1,0:T(8,128)(2,1)}, bf16[1024,320]{1,0:T(8,128)(2,1)}, bf16[1024,320]{1,0:T(8,128)(2,1)}) custom-call(bf16[8,1024,40]{2,1,0:T(8,128)(2,1)} %get-tuple-element.71.refs_0_, bf16[8,1024,40]{2,1,0:T(8,128)(2,1)} %get-tuple-element.72.refs_1_, bf16[8,1024,40]{2,1,0:T(8,128)(2,1)} %get-tuple-element.73.refs_2_, ...), custom_call_target="tpu_custom_call" | custom-call | tf_op jit(solution)/shard_map/pallas_call | solution.py:112
  199.8 33.0 %shard_map.125 = (bf16[2,8,864,128]{3,2,1,0:T(8,128)(2,1)}, bf16[2,8,240,128]{3,2,1,0:T(8,128)(2,1)}, f32[1,320]{1,0:T(1,128)}) custom-call(bf16[1024,320]{1,0:T(8,128)(2,1)} %get-tuple-element.84.refs_0_, bf16[1024,320]{1,0:T(8,128)(2,1)} %get-tuple-element.85.refs_1_, bf16[1024,320]{1,0:T(8,128)(2,1)} %get-tuple-element.86.refs_2_, ...), custom_call_target="tpu_custom_call" | custom-call | tf_op jit(solution)/shard_map/pallas_call | solution.py:112
  232.8 43.6 %shard_map.126 = (f32[856,128]{1,0:T(8,128)}, f32[856,128]{1,0:T(8,128)}, f32[16,40,128]{2,1,0:T(8,128)}) custom-call(bf16[2,8,864,128]{3,2,1,0:T(8,128)(2,1)} %get-tuple-element.106.p1, bf16[2,8,240,128]{3,2,1,0:T(8,128)(2,1)} %get-tuple-element.107.p0, f32[1,320]{1,0:T(1,128)} %get-tuple-element.108.dtv, bf16[4,1280,160]{2,1,0:T(8,128)(2,1)} %get-tuple-element.109.tw2_in, ...), custom_call_target="tpu_custom_call" | custom-call | tf_op jit(solution)/shard_map/pallas_call | solution.py:1309
  276.4 3.8 %shard_map.127 = (f32[2,856,128]{2,1,0:T(8,128)}, f32[2,856,128]{2,1,0:T(8,128)}, f32[2,856,128]{2,1,0:T(8,128)}, f32[1,1]{1,0:T(1,128)}, f32[1,1]{1,0:T(1,128)}) custom-call(f32[2,856,128]{2,1,0:T(8,128)} %bitcast.16, f32[2,856,128]{2,1,0:T(8,128)} %bitcast.17, f32[2,856,128]{2,1,0:T(8,128)} %bitcast.18, f32[856,128]{1,0:T(8,128)} %get-tuple-element.115.refs_3_, ...), custom_call_target="tpu_custom_call" | custom-call | tf_op jit(solution)/shard_map/pallas_call | solution.py:112

commit v2 on v1

--- a/solution.py
+++ b/solution.py
@@ -1075,7 +1075,7 @@
         time_last,
         both(rows_of_taps[2], outs[4].start),
     ]
-    ahead = 4
+    ahead = 2
     for i in range(ahead):
         begin(i)
     e[...] = jnp.broadcast_to(time_features(step[...]), (8, D))

time: 285 us -> 282 us (0.989)
  no operation moved by 1% of the time
where the time goes in v2:
time: 282 us; the launch traced here: 280 us
  Pallas kernels  278 us (99%)
    pallas_call x7, Pallas kernels, kcall(): pl.pallas_call(whole, out_shape=outs, in_specs=[hbm if i in late else vm...  158 us
    pallas_call x1, Pallas kernels, gather_weights(): pl.pallas_call(gather_kernel, out_shape=(gathered, gathered) + small + la...  75.8 us
    pallas_call x1, Pallas kernels, sum_over_samples(): pl.pallas_call(reduce_kernel, out_shape=(sds((ROWS, 128)), sds((ROWS, 128...  44.6 us

profile of v2, /device:TPU:1, one launch (start us, length us, event | category | flops | bytes accessed | tf_op | source)
XLA Modules:
  0.0 279.5 jit_solution(4689938360107733595)
XLA Ops:
  1.3 75.8 %shard_map.119 = (bf16[2,4,2,2,864,128]{5,4,3,2,1,0:T(8,128)(2,1)}, bf16[2,4,2,2,864,128]{5,4,3,2,1,0:T(8,128)(2,1)}, f32[8,320]{1,0:T(8,128)}, f32[4,1024]{1,0:...) custom-call(f32[2,856,128]{2,1,0:T(8,128)} %bitcast.15, ...), custom_call_target="tpu_custom_call" | custom-call | tf_op jit(solution)/shard_map/pallas_call | solution.py:1115
  77.0 15.1 %shard_map.120 = (bf16[3,960,320]{2,1,0:T(8,128)(2,1)}, bf16[3,320,960]{2,1,0:T(8,128)(2,1)}, bf16[4,320,320]{2,1,0:T(8,128)(2,1)}, bf16[16,320,320]{2,1,0:T(8,1...) custom-call(bf16[2,16,864,128]{3,2,1,0:T(8,128)(2,1)} %bitcast.14), custom_call_target="tpu_custom_call" | custom-call | tf_op jit(solution)/shard_map/pallas_call | solution.py:112
  92.2 14.6 %shard_map.121 = (f32[1024,320]{1,0:T(8,128)}, f32[1024,320]{1,0:T(8,128)}, bf16[1024,320]{1,0:T(8,128)(2,1)}, bf16[1024,320]{1,0:T(8,128)(2,1)}, bf16[1024,320]...) custom-call(f32[1024,320]{1,0:T(8,128)} %get-tuple-element.64.refs_0, ...), custom_call_target="tpu_custom_call" | custom-call | tf_op jit(solution)/shard_map/pallas_call | solution.py:112
  106.8 16.3 %shard_map.122 = (bf16[1024,320]{1,0:T(8,128)(2,1)}, f32[8,1,1024]{2,1,0:T(1,128)}) custom-call(bf16[8,1024,40]{2,1,0:T(8,128)(2,1)} %get-tuple-element.71.refs_0_, bf16[8,1024,40]{2,1,0:T(8,128)(2,1)} %get-tuple-element.72.refs_1_, bf16[8,1024,40]{2,1,0:T(8,128)(2,1)} %get-tuple-element.73.refs_2_), custom_call_target="tpu_custom_call" | custom-call | tf_op jit(solution)/shard_map/pallas_call | solution.py:112
  123.1 45.0 %shard_map.123 = (f32[1024,320]{1,0:T(8,128)}, f32[1024,320]{1,0:T(8,128)}, bf16[8,1024,40]{2,1,0:T(8,128)(2,1)}, f32[1,1]{1,0:T(1,128)}, bf16[4,320,160]{2,1,0:...) custom-call(bf16[1024,320]{1,0:T(8,128)(2,1)} %get-tuple-element.74., ...), custom_call_target="tpu_custom_call" | custom-call | tf_op jit(solution)/shard_map/pallas_call | solution.py:112
  168.2 29.8 %shard_map.124 = (bf16[1024,320]{1,0:T(8,128)(2,1)}, bf16[1024,320]{1,0:T(8,128)(2,1)}, bf16[1024,320]{1,0:T(8,128)(2,1)}) custom-call(bf16[8,1024,40]{2,1,0:T(8,128)(2,1)} %get-tuple-element.71.refs_0_, bf16[8,1024,40]{2,1,0:T(8,128)(2,1)} %get-tuple-element.72.refs_1_, bf16[8,1024,40]{2,1,0:T(8,128)(2,1)} %get-tuple-element.73.refs_2_, ...), custom_call_target="tpu_custom_call" | custom-call | tf_op jit(solution)/shard_map/pallas_call | solution.py:112
  197.9 33.0 %shard_map.125 = (bf16[2,8,864,128]{3,2,1,0:T(8,128)(2,1)}, bf16[2,8,240,128]{3,2,1,0:T(8,128)(2,1)}, f32[1,320]{1,0:T(1,128)}) custom-call(bf16[1024,320]{1,0:T(8,128)(2,1)} %get-tuple-element.84.refs_0_, bf16[1024,320]{1,0:T(8,128)(2,1)} %get-tuple-element.85.refs_1_, bf16[1024,320]{1,0:T(8,128)(2,1)} %get-tuple-element.86.refs_2_, ...), custom_call_target="tpu_custom_call" | custom-call | tf_op jit(solution)/shard_map/pallas_call | solution.py:112
  230.9 44.6 %shard_map.126 = (f32[856,128]{1,0:T(8,128)}, f32[856,128]{1,0:T(8,128)}, f32[16,40,128]{2,1,0:T(8,128)}) custom-call(bf16[2,8,864,128]{3,2,1,0:T(8,128)(2,1)} %get-tuple-element.106.p1, bf16[2,8,240,128]{3,2,1,0:T(8,128)(2,1)} %get-tuple-element.107.p0, f32[1,320]{1,0:T(1,128)} %get-tuple-element.108.dtv, bf16[4,1280,160]{2,1,0:T(8,128)(2,1)} %get-tuple-element.109.tw2_in, ...), custom_call_target="tpu_custom_call" | custom-call | tf_op jit(solution)/shard_map/pallas_call | solution.py:1309
  275.5 3.8 %shard_map.127 = (f32[2,856,128]{2,1,0:T(8,128)}, f32[2,856,128]{2,1,0:T(8,128)}, f32[2,856,128]{2,1,0:T(8,128)}, f32[1,1]{1,0:T(1,128)}, f32[1,1]{1,0:T(1,128)}) custom-call(f32[2,856,128]{2,1,0:T(8,128)} %bitcast.16, f32[2,856,128]{2,1,0:T(8,128)} %bitcast.17, f32[2,856,128]{2,1,0:T(8,128)} %bitcast.18, f32[856,128]{1,0:T(8,128)} %get-tuple-element.115.refs_3_, ...), custom_call_target="tpu_custom_call" | custom-call | tf_op jit(solution)/shard_map/pallas_call | solution.py:112
